TPU v7x, 128 devices: a whole 4x4x4 slice. The times are simulated.
128 devices in a mesh: gx: 8 (over z, core), gy: 16 (over x, y).
Axes of the slice: x: 4, y: 4, z: 4, core: 2. Of those that a mesh axis runs over, the one named last changes fastest.
Arguments:
- view_tiles: bfloat16 [49152, 32, 128], P(('gx', 'gy')), may hold values from 0.19921875 to 5
- tile_owner: int32 [49152], P(('gx', 'gy')), may hold values from 0 to 127, as said below
- tile_offset: int32 [49152], P(('gx', 'gy')), may hold values from 0 to 383, as said below
- estimate: float32 [512, 512, 128], P('gx', 'gy'), may hold values from 0.5 to 2
- spread_taps: float32 [6, 3, 31], replicated, may hold values from 0.05 to 1
Outputs:
- updated: float32 [512, 512, 128], P('gx', 'gy')
Inputs may be any that keep to these rules, and one draw needn't show every extreme that they name: `tile_owner`: the owner of every tile is the device at most one step away along gx and at most one step along gy from the device that holds the tile, counted around the device grid; no device sends more than 64 tiles to one owner, and every device sends exactly 64 to some owner; every owner receives exactly 384 tiles in all. `tile_offset`: over the tiles of one owner the offsets are all of 0 to 383, each once.
All inputs are finite; a program needn't handle non-finite values.
Results may differ from a plain program's by a relative error of at most 0.001.
Values may be sent and summed in bfloat16 or wider, within the bound.
A program may use at most 128 MiB of HBM per device.

v0:
```python
import jax
import jax.numpy as jnp
from jax import lax
from jax.experimental import pallas as pl
from jax.experimental.pallas import tpu as pltpu
from jax.sharding import PartitionSpec as P

MESH = pl.DeviceIdType.MESH
F32, BF16, I32 = jnp.float32, jnp.bfloat16, jnp.int32

VIEWS, TAPS = 6, 31
ROWS, COLS, DEPTH = 64, 32, 128
TILES = 384
HALO = 16
XROWS, XCOLS = ROWS + 2 * HALO, COLS + 2 * HALO
SLOTS = 64
OWN = 4
ORDER = (5, 3, 2, 0, 8, 6, 1, 7)
BANDS = XROWS // 16
TILE_BANDS = ROWS // 16


def dot(a, b):
    return jnp.dot(a, b, preferred_element_type=F32)


def dot_nt(a, b):
    return lax.dot_general(a, b, (((1,), (1,)), ((), ())), preferred_element_type=F32)


def iota(shape, dim):
    return lax.broadcasted_iota(I32, shape, dim)


def onehot(mask):
    return jnp.where(mask, 1.0, 0.0).astype(BF16)


def shifted_rows(row, rows, shift):
    wide = jnp.broadcast_to(row, (rows, row.shape[1]))
    return pltpu.roll(wide, shift, 1, stride=1, stride_axis=0)


def lanes(a, b):
    return jnp.concatenate([a, b], axis=1)


def kernel(
    nx, ny,
    taps_ref, owner_ref, offset_ref, est_hbm, tiles_hbm,
    out_ref,
    est_v, tiles_v, packed, arrived, ext, blurred, recip, quot, back_rows,
    center, side_out, side_in, row_out, row_in,
    kpad, row_fwd, row_bwd, col_fwd, col_bwd, depth_fwd, depth_bwd,
    index_v, index_s, slot_v, slot_s, label_out, label_in,
    load_sem, index_sem,
    halo_send, halo_recv, tile_send, tile_recv, label_send, label_recv,
    side_send, side_recv, row_send, row_recv,
):
    gx, gy = lax.axis_index("gx"), lax.axis_index("gy")

    def device(dx, dy):
        return (lax.rem(gx + dx + nx, nx), lax.rem(gy + dy + ny, ny))

    def step_of(group):
        return group // 3 - 1, group % 3 - 1

    load_est = pltpu.make_async_copy(est_hbm, est_v, load_sem.at[0])
    load_tiles = pltpu.make_async_copy(tiles_hbm, tiles_v, load_sem.at[1])
    load_est.start()
    load_tiles.start()

    barrier = pltpu.get_barrier_semaphore()
    for group in ORDER:
        pl.semaphore_signal(barrier, inc=1, device_id=device(*step_of(group)), device_id_type=MESH)

    load_est.wait()
    zero_row = jnp.zeros((XCOLS, DEPTH), BF16)
    ext[0] = zero_row
    ext[XROWS - 1] = zero_row
    ext[HALO:HALO + ROWS, HALO:HALO + COLS, :] = est_v[...].astype(BF16)
    pl.semaphore_wait(barrier, len(ORDER))

    def part(step, size):
        if step > 0:
            return (size, size + HALO), (0, HALO)
        if step < 0:
            return (HALO, 2 * HALO), (size + HALO, size + 2 * HALO)
        return (HALO, HALO + size), (HALO, HALO + size)

    halo_copies = []
    for group in ORDER:
        dx, dy = step_of(group)
        (r0, r1), (s0, s1) = part(dx, ROWS)
        if dx > 0:
            r0, s0 = r0 + 1, s0 + 1
        if dx < 0:
            r1, s1 = r1 - 1, s1 - 1
        (c0, c1), (d0, d1) = part(dy, COLS)
        copy = pltpu.make_async_remote_copy(
            src_ref=ext.at[r0:r1, c0:c1, :],
            dst_ref=ext.at[s0:s1, d0:d1, :],
            send_sem=halo_send.at[group],
            recv_sem=halo_recv.at[group],
            device_id=device(dx, dy),
            device_id_type=MESH,
        )
        copy.start()
        halo_copies.append(copy)

    owner = owner_ref[...]
    shift = ny.bit_length() - 1

    def wrapped(d, n):
        return jnp.where(d == 0, 1, jnp.where(d == 1, 2, jnp.where(d == 1 - n, 2, 0)))

    group_of = wrapped((owner >> shift) - gx, nx) * 3 + wrapped((owner & (ny - 1)) - gy, ny)
    members = jnp.where(iota((16, TILES), 0) == group_of, 1.0, 0.0)
    before = onehot(iota((TILES, TILES), 0) < iota((TILES, TILES), 1))
    rank = jnp.sum(members * dot(members.astype(BF16), before), axis=0, keepdims=True)
    place = group_of * 128 + rank.astype(I32)
    picks = onehot(iota((9 * 128, TILES), 0) == place)
    number = iota((8, TILES), 1)
    row = iota((8, TILES), 0)
    offset = jnp.broadcast_to(offset_ref[...], (8, TILES))
    digits = jnp.where(row == 0, number >> 4, jnp.where(row == 1, number & 15, jnp.where(
        row == 2, offset >> 4, jnp.where(row == 3, offset & 15, 1))))
    found = dot_nt(digits.astype(F32).astype(BF16), picks)
    source = jnp.clip((found[0:1] * 16.0 + found[1:2]).astype(I32), 0, TILES - 1)
    label = (found[2:3] * 16.0 + found[3:4] + (found[4:5] - 1.0) * 1024.0).astype(I32)
    index_v[...] = jnp.zeros_like(index_v)
    for group in range(9):
        index_v[group:group + 1, :] = source[:, group * 128:(group + 1) * 128]
        label_out[group] = jnp.broadcast_to(label[:, group * 128:(group + 1) * 128], (8, 128))
    load_index = pltpu.make_async_copy(index_v, index_s, index_sem.at[0])
    load_index.start()
    label_copies = []
    for group in ORDER:
        copy = pltpu.make_async_remote_copy(
            src_ref=label_out.at[group],
            dst_ref=label_in.at[group],
            send_sem=label_send.at[group],
            recv_sem=label_recv.at[group],
            device_id=device(*step_of(group)),
            device_id_type=MESH,
        )
        copy.start()
        label_copies.append(copy)
    label_in[OWN] = label_out[OWN]

    load_index.wait()
    load_tiles.wait()
    tile_copies = []
    for group in ORDER:
        def pack(r, carry, group=group):
            packed[group * SLOTS + r] = tiles_v[index_s[group, r]]
            return carry

        lax.fori_loop(0, SLOTS, pack, 0, unroll=8)
        copy = pltpu.make_async_remote_copy(
            src_ref=packed.at[group * SLOTS:(group + 1) * SLOTS],
            dst_ref=arrived.at[group * SLOTS:(group + 1) * SLOTS],
            send_sem=tile_send.at[group],
            recv_sem=tile_recv.at[group],
            device_id=device(*step_of(group)),
            device_id_type=MESH,
        )
        copy.start()
        tile_copies.append(copy)

    def keep(r, carry):
        arrived[OWN * SLOTS + r] = tiles_v[index_s[OWN, r]]
        return carry

    lax.fori_loop(0, SLOTS, keep, 0, unroll=8)

    kpad[...] = jnp.zeros_like(kpad)
    kpad[:, 0:3, 0:TAPS] = taps_ref[...]
    spread = onehot((iota((256, 16), 0) >> 4) == iota((256, 16), 1))
    spread_wide = onehot((iota((768, 128), 0) >> 4) == iota((768, 128), 1))
    same = (iota((256, 256), 0) & 15) == (iota((256, 256), 1) & 15)
    eye = onehot(iota((128, 128), 0) == iota((128, 128), 1))
    depth_fwd[...] = jnp.zeros_like(depth_fwd)
    depth_bwd[...] = jnp.zeros_like(depth_bwd)
    for v in range(VIEWS):
        raw = kpad[v][0:3]
        norm = raw / jnp.sum(raw, axis=1, keepdims=True)
        rows_band = shifted_rows(norm[0:1], 16, 1).astype(BF16)
        wide = dot(spread, rows_band).astype(BF16)
        for d in range(3):
            fwd = dot_nt(wide, spread_wide[256 * d:256 * (d + 1)])
            row_fwd[v, :, 256 * d:256 * (d + 1)] = jnp.where(same, fwd, 0.0).astype(BF16)
            tall = dot_nt(spread_wide[256 * d:256 * (d + 1)], rows_band).astype(BF16)
            bwd = dot_nt(tall, spread)
            row_bwd[v, :, 256 * (2 - d):256 * (3 - d)] = jnp.where(same, bwd, 0.0).astype(BF16)
        cols_band = shifted_rows(norm[1:2], COLS, 1)
        col_fwd[v * COLS:(v + 1) * COLS, :] = cols_band.astype(BF16)
        long = lanes(norm[2:3], jnp.zeros((1, 128), F32))
        depth_t = shifted_rows(long, DEPTH, 128 - TAPS // 2)[:, 128:256].astype(BF16)
        at = slice(128 * (v % 2), 128 * (v % 2) + 128)
        depth_bwd[v // 2, at, at] = depth_t
        depth_fwd[v // 2, at, at] = dot_nt(eye, depth_t).astype(BF16)
    col_bwd[...] = dot_nt(eye[0:XCOLS], col_fwd[...]).astype(BF16)

    for copy in halo_copies:
        copy.wait_recv()

    def clear(edge, rows, cols):
        @pl.when(edge)
        def _():
            ext[rows, cols, :] = jnp.zeros((rows.stop - rows.start, cols.stop - cols.start, DEPTH), BF16)

    every_row, every_col = slice(0, XROWS), slice(0, XCOLS)
    clear(gx == 0, slice(0, HALO), every_col)
    clear(gx == nx - 1, slice(XROWS - HALO, XROWS), every_col)
    clear(gy == 0, every_row, slice(0, HALO))
    clear(gy == ny - 1, every_row, slice(XCOLS - HALO, XCOLS))

    def columns(p, carry):
        a = 2 * p
        both = lanes(ext[a], ext[a + 1])
        out = dot(col_fwd[:, 0:XCOLS], both).astype(BF16)
        blurred[a] = out[:, 0:128].reshape(VIEWS, COLS, DEPTH)
        blurred[a + 1] = out[:, 128:256].reshape(VIEWS, COLS, DEPTH)
        return carry

    lax.fori_loop(0, XROWS // 2, columns, 0)

    def rows_depth(n, carry):
        band, pair = n // 3, n % 3
        first = pl.multiple_of(band * 16, 16)
        parts = []
        for e in range(2):
            block = blurred[pl.ds(first, 48), 2 * pair + e]
            both = lanes(block[:, 0:16].reshape(768, DEPTH), block[:, 16:32].reshape(768, DEPTH))
            parts.append(dot(row_fwd[2 * pair + e], both).astype(BF16))
        for h in range(2):
            both = lanes(parts[0][:, 128 * h:128 * h + 128], parts[1][:, 128 * h:128 * h + 128])
            inverse = 1.0 / dot(both, depth_fwd[pair])
            for e in range(2):
                recip[2 * pair + e, pl.ds(first, 16), 16 * h:16 * h + 16, :] = inverse[
                    :, 128 * e:128 * e + 128].reshape(16, 16, DEPTH)
        return carry

    lax.fori_loop(0, TILE_BANDS * 3, rows_depth, 0)

    for copy in label_copies:
        copy.wait_recv()
    labels = jnp.concatenate([label_in[group][0:1] for group in range(9)], axis=1)
    where_is = onehot(iota((TILES, 9 * 128), 0) == labels)
    place_no = iota((8, 9 * 128), 1)
    place_digits = jnp.where(iota((8, 9 * 128), 0) == 0, place_no >> 7, place_no & 127)
    got = dot_nt(place_digits.astype(F32).astype(BF16), where_is)
    slots = jnp.clip((got[0:1] * float(SLOTS) + got[1:2]).astype(I32), 0, 9 * SLOTS - 1)
    slot_v[...] = jnp.zeros_like(slot_v)
    for n in range(3):
        slot_v[n:n + 1, :] = slots[:, 128 * n:128 * (n + 1)]
    load_slots = pltpu.make_async_copy(slot_v, slot_s, index_sem.at[1])
    load_slots.start()
    load_slots.wait()
    for copy in tile_copies:
        copy.wait_recv()

    side_copies, row_copies = [], []
    for band in range(BANDS):
        if band < TILE_BANDS:
            def quotients(pair, carry, band=band):
                tiles = []
                for i in range(16):
                    halves = []
                    for e in range(2):
                        at = slot_s[pair, 64 * e + 16 * band + i]
                        value = arrived[at].astype(F32) * recip[2 * pair + e, 16 * band + i]
                        halves.append(value.astype(BF16))
                    tiles.append(lanes(halves[0], halves[1]))
                out = dot(jnp.concatenate(tiles, axis=0), depth_bwd[pair]).astype(BF16)
                for e in range(2):
                    quot[2 * pair + e, 16 * band:16 * band + 16] = out[
                        :, 128 * e:128 * e + 128].reshape(16, COLS, DEPTH)
                return carry

            lax.fori_loop(0, 3, quotients, 0)
        s0, s1 = max(0, band - 2), min(TILE_BANDS - 1, band)
        w0, w1 = 256 * (2 - (band - s0)), 256 * (3 - (band - s1))

        def rows_back(v, carry, s0=s0, s1=s1, w0=w0, w1=w1):
            block = quot[v, 16 * s0:16 * (s1 + 1)]
            both = lanes(block[:, 0:16].reshape(w1 - w0, DEPTH), block[:, 16:32].reshape(w1 - w0, DEPTH))
            out = dot(row_bwd[v, :, w0:w1], both).astype(BF16)
            back_rows[:, v, 0:16, :] = out[:, 0:128].reshape(16, 16, DEPTH)
            back_rows[:, v, 16:32, :] = out[:, 128:256].reshape(16, 16, DEPTH)
            return carry

        lax.fori_loop(0, VIEWS, rows_back, 0)

        def cols_back(p, carry, band=band):
            both = lanes(back_rows[2 * p].reshape(VIEWS * COLS, DEPTH), back_rows[2 * p + 1].reshape(VIEWS * COLS, DEPTH))
            out = dot(col_bwd[...], both)
            for e in range(2):
                one = out[:, 128 * e:128 * e + 128]
                side_out[band, 0, 2 * p + e] = one[0:HALO].astype(BF16)
                side_out[band, 1, 2 * p + e] = one[HALO + COLS:XCOLS].astype(BF16)
                mid = one[HALO:HALO + COLS]
                if 1 <= band <= TILE_BANDS:
                    center[16 * (band - 1) + 2 * p + e] = mid
                else:
                    row_out[band // (BANDS - 1), 2 * p + e] = mid.astype(BF16)
            return carry

        lax.fori_loop(0, 8, cols_back, 0)
        dx = -1 if band == 0 else 1 if band == BANDS - 1 else 0
        for side in range(2):
            copy = pltpu.make_async_remote_copy(
                src_ref=side_out.at[band, side],
                dst_ref=side_in.at[band, side],
                send_sem=side_send.at[band, side],
                recv_sem=side_recv.at[band, side],
                device_id=device(dx, 2 * side - 1),
                device_id_type=MESH,
            )
            copy.start()
            side_copies.append(copy)
        if dx != 0:
            end = band // (BANDS - 1)
            copy = pltpu.make_async_remote_copy(
                src_ref=row_out.at[end],
                dst_ref=row_in.at[end],
                send_sem=row_send.at[end],
                recv_sem=row_recv.at[end],
                device_id=device(dx, 0),
                device_id_type=MESH,
            )
            copy.start()
            row_copies.append(copy)

    for copy in side_copies + row_copies:
        copy.wait_recv()

    from_right, from_left = gy != ny - 1, gy != 0
    for c in range(TILE_BANDS):
        rows = slice(16 * c, 16 * c + 16)

        def sides(band, inside):
            low = side_in[band, 1].astype(F32)
            high = side_in[band, 0].astype(F32)
            return jnp.concatenate([
                jnp.where(jnp.logical_and(from_left, inside), low, 0.0),
                jnp.where(jnp.logical_and(from_right, inside), high, 0.0),
            ], axis=1)

        total = center[rows] + sides(c + 1, True)
        if c == 0:
            inside = gx != 0
            total = total + sides(BANDS - 1, inside) + jnp.where(inside, row_in[1].astype(F32), 0.0)
        if c == TILE_BANDS - 1:
            inside = gx != nx - 1
            total = total + sides(0, inside) + jnp.where(inside, row_in[0].astype(F32), 0.0)
        out_ref[rows] = total

    for copy in halo_copies + label_copies + tile_copies + side_copies + row_copies:
        copy.wait_send()


def body(view_tiles, tile_owner, tile_offset, estimate, spread_taps):
    nx, ny = lax.axis_size("gx"), lax.axis_size("gy")
    vmem = pl.BlockSpec(memory_space=pltpu.VMEM)
    anywhere = pl.BlockSpec(memory_space=pl.ANY)
    dma = pltpu.SemaphoreType.DMA
    total = pl.pallas_call(
        lambda *refs: kernel(nx, ny, *refs),
        out_shape=jax.ShapeDtypeStruct((ROWS, COLS, DEPTH), F32),
        in_specs=[vmem, vmem, vmem, anywhere, anywhere],
        out_specs=vmem,
        scratch_shapes=[
            pltpu.VMEM((ROWS, COLS, DEPTH), F32),
            pltpu.VMEM((TILES, COLS, DEPTH), BF16),
            pltpu.VMEM((9 * SLOTS, COLS, DEPTH), BF16),
            pltpu.VMEM((9 * SLOTS, COLS, DEPTH), BF16),
            pltpu.VMEM((XROWS, XCOLS, DEPTH), BF16),
            pltpu.VMEM((XROWS, VIEWS, COLS, DEPTH), BF16),
            pltpu.VMEM((VIEWS, ROWS, COLS, DEPTH), F32),
            pltpu.VMEM((VIEWS, ROWS, COLS, DEPTH), BF16),
            pltpu.VMEM((16, VIEWS, COLS, DEPTH), BF16),
            pltpu.VMEM((ROWS, COLS, DEPTH), F32),
            pltpu.VMEM((BANDS, 2, 16, HALO, DEPTH), BF16),
            pltpu.VMEM((BANDS, 2, 16, HALO, DEPTH), BF16),
            pltpu.VMEM((2, 16, COLS, DEPTH), BF16),
            pltpu.VMEM((2, 16, COLS, DEPTH), BF16),
            pltpu.VMEM((VIEWS, 8, 128), F32),
            pltpu.VMEM((VIEWS, 256, 768), BF16),
            pltpu.VMEM((VIEWS, 256, 768), BF16),
            pltpu.VMEM((VIEWS * COLS, 128), BF16),
            pltpu.VMEM((XCOLS, VIEWS * COLS), BF16),
            pltpu.VMEM((VIEWS // 2, 256, 256), BF16),
            pltpu.VMEM((VIEWS // 2, 256, 256), BF16),
            pltpu.VMEM((16, 128), I32),
            pltpu.SMEM((16, 128), I32),
            pltpu.VMEM((8, 128), I32),
            pltpu.SMEM((8, 128), I32),
            pltpu.VMEM((9, 8, 128), I32),
            pltpu.VMEM((9, 8, 128), I32),
            dma((2,)), dma((2,)),
            dma((9,)), dma((9,)), dma((9,)), dma((9,)), dma((9,)), dma((9,)),
            dma((BANDS, 2)), dma((BANDS, 2)), dma((2,)), dma((2,)),
        ],
        compiler_params=pltpu.CompilerParams(
            collective_id=0, has_side_effects=True, vmem_limit_bytes=56 * 1024 * 1024
        ),
        name="richardson_lucy",
    )(spread_taps, tile_owner.reshape(1, TILES), tile_offset.reshape(1, TILES), estimate, view_tiles)
    return estimate * (total / VIEWS)


def solution(mesh):
    placed = (
        P(("gx", "gy"), None, None),
        P(("gx", "gy")),
        P(("gx", "gy")),
        P("gx", "gy", None),
        P(),
    )
    return jax.shard_map(
        body, mesh=mesh, in_specs=placed, out_specs=P("gx", "gy", None), check_vma=False
    )
```

profile of v0, /device:TPU:1, one launch (start us, length us, event | category | flops | bytes accessed | tf_op | source)
XLA Modules:
  0.0 86.1 jit_solution(12134240636182475513)
XLA Ops:
  0.0 0.0 copy-start
  0.0 1.3 %reshape.6.refs_1_ = s32[1,384]{1,0:T(1,128)} reshape(s32[384]{0:T(512)} %param.6) | data formatting | bytes 3072 | tf_op jit(solution)/shard_map/reshape | solution.py:410
  1.3 1.3 %reshape.7.refs_2_ = s32[1,384]{1,0:T(1,128)} reshape(s32[384]{0:T(512)} %param.7) | data formatting | bytes 3072 | tf_op jit(solution)/shard_map/reshape | solution.py:410
  2.6 81.1 %richardson_lucy.1 = f32[64,32,128]{2,1,0:T(8,128)} custom-call(f32[6,3,31]{2,1,0:T(4,128)} %refs_0_.1, s32[1,384]{1,0:T(1,128)} %reshape.6.refs_1_, s32[1,384]{1,0:T(1,128)} %reshape.7.refs_2_, f32[64,32,128]{2,1,0:T(8,128)} %refs_3_.1, bf16[384,32,128]{2,1,0:T(8,128)(2,1)} %refs_4_.1), custom_call_target="tpu_custom_call" | custom-call | tf_op jit(solution)/shard_map/richardson_lucy/pallas_call | solution.py:369
  83.7 0.0 copy-done
  83.7 2.4 %multiply_multiply_fusion = f32[64,32,128]{2,1,0:T(8,128)} fusion(f32[64,32,128]{2,1,0:T(8,128)S(1)} %copy-done, f32[64,32,128]{2,1,0:T(8,128)} %richardson_lucy.1), kind=kLoop, calls=%fused_computation | loop fusion | flops 524288 | bytes 3145728 | tf_op jit(solution)/shard_map/mul | solution.py:411
Async XLA Ops:
  0.0 83.7 %copy-start = (f32[64,32,128]{2,1,0:T(8,128)S(1)}, f32[64,32,128]{2,1,0:T(8,128)}, u32[]{:S(2)}) copy-start(f32[64,32,128]{2,1,0:T(8,128)} %refs_3_.1) | copy-start | bytes 3145732
where the time goes:
time: 86.4 us; the launch traced here: 86.1 us
  Pallas kernels  81.1 us (94%)
  local copies, waits for them, and re-layouts  2.61 us (3%)
  other arithmetic  2.42 us (3%)
    pallas_call x1, Pallas kernels, body(): pl.pallas_call(lambda *refs: kernel(nx, ny, *refs), out_shape=jax.ShapeDt...  81.1 us
    mul x1, other arithmetic, body(): return estimate * (total / VIEWS)  2.42 us

commit v1 on v0

--- a/solution.py
+++ b/solution.py
@@ -53,7 +53,7 @@
     center, side_out, side_in, row_out, row_in,
     kpad, row_fwd, row_bwd, col_fwd, col_bwd, depth_fwd, depth_bwd,
     index_v, index_s, slot_v, slot_s, label_out, label_in,
-    load_sem, index_sem,
+    load_sem, index_sem, store_sem,
     halo_send, halo_recv, tile_send, tile_recv, label_send, label_recv,
     side_send, side_recv, row_send, row_recv,
 ):
@@ -81,34 +81,25 @@
     ext[HALO:HALO + ROWS, HALO:HALO + COLS, :] = est_v[...].astype(BF16)
     pl.semaphore_wait(barrier, len(ORDER))
 
-    def part(step, size):
-        if step > 0:
-            return (size, size + HALO), (0, HALO)
-        if step < 0:
-            return (HALO, 2 * HALO), (size + HALO, size + 2 * HALO)
-        return (HALO, HALO + size), (HALO, HALO + size)
-
-    halo_copies = []
-    for group in ORDER:
-        dx, dy = step_of(group)
-        (r0, r1), (s0, s1) = part(dx, ROWS)
-        if dx > 0:
-            r0, s0 = r0 + 1, s0 + 1
-        if dx < 0:
-            r1, s1 = r1 - 1, s1 - 1
-        (c0, c1), (d0, d1) = part(dy, COLS)
+    def send_halo(group, src, dst):
         copy = pltpu.make_async_remote_copy(
-            src_ref=ext.at[r0:r1, c0:c1, :],
-            dst_ref=ext.at[s0:s1, d0:d1, :],
+            src_ref=ext.at[src],
+            dst_ref=ext.at[dst],
             send_sem=halo_send.at[group],
             recv_sem=halo_recv.at[group],
-            device_id=device(dx, dy),
+            device_id=device(*step_of(group)),
             device_id_type=MESH,
         )
         copy.start()
-        halo_copies.append(copy)
-
-    owner = owner_ref[...]
+        return copy
+
+    inner = slice(HALO, HALO + ROWS)
+    halo_copies = [
+        send_halo(5, (inner, slice(COLS, COLS + HALO)), (inner, slice(0, HALO))),
+        send_halo(3, (inner, slice(HALO, 2 * HALO)), (inner, slice(HALO + COLS, XCOLS))),
+    ]
+
+    owner = owner_ref[...].reshape(1, TILES)
     shift = ny.bit_length() - 1
 
     def wrapped(d, n):
@@ -122,7 +113,7 @@
     picks = onehot(iota((9 * 128, TILES), 0) == place)
     number = iota((8, TILES), 1)
     row = iota((8, TILES), 0)
-    offset = jnp.broadcast_to(offset_ref[...], (8, TILES))
+    offset = jnp.broadcast_to(offset_ref[...].reshape(1, TILES), (8, TILES))
     digits = jnp.where(row == 0, number >> 4, jnp.where(row == 1, number & 15, jnp.where(
         row == 2, offset >> 4, jnp.where(row == 3, offset & 15, 1))))
     found = dot_nt(digits.astype(F32).astype(BF16), picks)
@@ -173,6 +164,20 @@
         return carry
 
     lax.fori_loop(0, SLOTS, keep, 0, unroll=8)
+
+    def clear(edge, rows, cols):
+        @pl.when(edge)
+        def _():
+            ext[rows, cols, :] = jnp.zeros((rows.stop - rows.start, cols.stop - cols.start, DEPTH), BF16)
+
+    for copy in halo_copies:
+        copy.wait_recv()
+    clear(gy == 0, inner, slice(0, HALO))
+    clear(gy == ny - 1, inner, slice(HALO + COLS, XCOLS))
+    row_halos = [
+        send_halo(7, slice(ROWS + 1, ROWS + HALO), slice(1, HALO)),
+        send_halo(1, slice(HALO, 2 * HALO - 1), slice(HALO + ROWS, XROWS - 1)),
+    ]
 
     kpad[...] = jnp.zeros_like(kpad)
     kpad[:, 0:3, 0:TAPS] = taps_ref[...]
@@ -202,19 +207,11 @@
         depth_fwd[v // 2, at, at] = dot_nt(eye, depth_t).astype(BF16)
     col_bwd[...] = dot_nt(eye[0:XCOLS], col_fwd[...]).astype(BF16)
 
-    for copy in halo_copies:
+    for copy in row_halos:
         copy.wait_recv()
-
-    def clear(edge, rows, cols):
-        @pl.when(edge)
-        def _():
-            ext[rows, cols, :] = jnp.zeros((rows.stop - rows.start, cols.stop - cols.start, DEPTH), BF16)
-
-    every_row, every_col = slice(0, XROWS), slice(0, XCOLS)
-    clear(gx == 0, slice(0, HALO), every_col)
-    clear(gx == nx - 1, slice(XROWS - HALO, XROWS), every_col)
-    clear(gy == 0, every_row, slice(0, HALO))
-    clear(gy == ny - 1, every_row, slice(XCOLS - HALO, XCOLS))
+    halo_copies += row_halos
+    clear(gx == 0, slice(0, HALO), slice(0, XCOLS))
+    clear(gx == nx - 1, slice(XROWS - HALO, XROWS), slice(0, XCOLS))
 
     def columns(p, carry):
         a = 2 * p
@@ -224,7 +221,7 @@
         blurred[a + 1] = out[:, 128:256].reshape(VIEWS, COLS, DEPTH)
         return carry
 
-    lax.fori_loop(0, XROWS // 2, columns, 0)
+    lax.fori_loop(0, XROWS // 2, columns, 0, unroll=8)
 
     def rows_depth(n, carry):
         band, pair = n // 3, n % 3
@@ -242,7 +239,7 @@
                     :, 128 * e:128 * e + 128].reshape(16, 16, DEPTH)
         return carry
 
-    lax.fori_loop(0, TILE_BANDS * 3, rows_depth, 0)
+    lax.fori_loop(0, TILE_BANDS * 3, rows_depth, 0, unroll=3)
 
     for copy in label_copies:
         copy.wait_recv()
@@ -279,7 +276,7 @@
                         :, 128 * e:128 * e + 128].reshape(16, COLS, DEPTH)
                 return carry
 
-            lax.fori_loop(0, 3, quotients, 0)
+            lax.fori_loop(0, 3, quotients, 0, unroll=3)
         s0, s1 = max(0, band - 2), min(TILE_BANDS - 1, band)
         w0, w1 = 256 * (2 - (band - s0)), 256 * (3 - (band - s1))
 
@@ -291,7 +288,7 @@
             back_rows[:, v, 16:32, :] = out[:, 128:256].reshape(16, 16, DEPTH)
             return carry
 
-        lax.fori_loop(0, VIEWS, rows_back, 0)
+        lax.fori_loop(0, VIEWS, rows_back, 0, unroll=6)
 
         def cols_back(p, carry, band=band):
             both = lanes(back_rows[2 * p].reshape(VIEWS * COLS, DEPTH), back_rows[2 * p + 1].reshape(VIEWS * COLS, DEPTH))
@@ -307,7 +304,7 @@
                     row_out[band // (BANDS - 1), 2 * p + e] = mid.astype(BF16)
             return carry
 
-        lax.fori_loop(0, 8, cols_back, 0)
+        lax.fori_loop(0, 8, cols_back, 0, unroll=8)
         dx = -1 if band == 0 else 1 if band == BANDS - 1 else 0
         for side in range(2):
             copy = pltpu.make_async_remote_copy(
@@ -333,30 +330,37 @@
             copy.start()
             row_copies.append(copy)
 
-    for copy in side_copies + row_copies:
-        copy.wait_recv()
-
     from_right, from_left = gy != ny - 1, gy != 0
-    for c in range(TILE_BANDS):
+
+    def sides(band, inside):
+        for copy in side_copies[2 * band:2 * band + 2]:
+            copy.wait_recv()
+        low = side_in[band, 1].astype(F32)
+        high = side_in[band, 0].astype(F32)
+        return jnp.concatenate([
+            jnp.where(jnp.logical_and(from_left, inside), low, 0.0),
+            jnp.where(jnp.logical_and(from_right, inside), high, 0.0),
+        ], axis=1)
+
+    stores = []
+    for c in (1, 2, 0, 3):
         rows = slice(16 * c, 16 * c + 16)
-
-        def sides(band, inside):
-            low = side_in[band, 1].astype(F32)
-            high = side_in[band, 0].astype(F32)
-            return jnp.concatenate([
-                jnp.where(jnp.logical_and(from_left, inside), low, 0.0),
-                jnp.where(jnp.logical_and(from_right, inside), high, 0.0),
-            ], axis=1)
-
         total = center[rows] + sides(c + 1, True)
         if c == 0:
             inside = gx != 0
+            row_copies[1].wait_recv()
             total = total + sides(BANDS - 1, inside) + jnp.where(inside, row_in[1].astype(F32), 0.0)
         if c == TILE_BANDS - 1:
             inside = gx != nx - 1
+            row_copies[0].wait_recv()
             total = total + sides(0, inside) + jnp.where(inside, row_in[0].astype(F32), 0.0)
-        out_ref[rows] = total
-
+        center[rows] = est_v[rows] * (total * (1.0 / VIEWS))
+        store = pltpu.make_async_copy(center.at[rows], out_ref.at[rows], store_sem.at[c])
+        store.start()
+        stores.append(store)
+
+    for store in stores:
+        store.wait()
     for copy in halo_copies + label_copies + tile_copies + side_copies + row_copies:
         copy.wait_send()
 
@@ -366,11 +370,11 @@
     vmem = pl.BlockSpec(memory_space=pltpu.VMEM)
     anywhere = pl.BlockSpec(memory_space=pl.ANY)
     dma = pltpu.SemaphoreType.DMA
-    total = pl.pallas_call(
+    return pl.pallas_call(
         lambda *refs: kernel(nx, ny, *refs),
         out_shape=jax.ShapeDtypeStruct((ROWS, COLS, DEPTH), F32),
         in_specs=[vmem, vmem, vmem, anywhere, anywhere],
-        out_specs=vmem,
+        out_specs=anywhere,
         scratch_shapes=[
             pltpu.VMEM((ROWS, COLS, DEPTH), F32),
             pltpu.VMEM((TILES, COLS, DEPTH), BF16),
@@ -399,7 +403,7 @@
             pltpu.SMEM((8, 128), I32),
             pltpu.VMEM((9, 8, 128), I32),
             pltpu.VMEM((9, 8, 128), I32),
-            dma((2,)), dma((2,)),
+            dma((2,)), dma((2,)), dma((4,)),
             dma((9,)), dma((9,)), dma((9,)), dma((9,)), dma((9,)), dma((9,)),
             dma((BANDS, 2)), dma((BANDS, 2)), dma((2,)), dma((2,)),
         ],
@@ -407,8 +411,7 @@
             collective_id=0, has_side_effects=True, vmem_limit_bytes=56 * 1024 * 1024
         ),
         name="richardson_lucy",
-    )(spread_taps, tile_owner.reshape(1, TILES), tile_offset.reshape(1, TILES), estimate, view_tiles)
-    return estimate * (total / VIEWS)
+    )(spread_taps, tile_owner, tile_offset, estimate, view_tiles)
 
 
 def solution(mesh):

time: 86.4 us -> 69.8 us (0.81)
  Pallas kernels: 81.1 us -> 67.3 us
  other arithmetic: 2.42 us -> 0 us
    pallas_call x1, Pallas kernels: 81.1 us -> 67.3 us  [body(): pl.pallas_call(lambda *refs: kernel(nx, ny, *refs), out_shape=jax.ShapeDt...]
    reshape x2 -> x0, local copies, waits for them, and re-layouts: 2.61 us -> none  [the longest x1 1.33 us: body(): tile_owner.reshape(1, TILES)]
    mul x1 -> x0, other arithmetic: 2.42 us -> none  [body(): return estimate * (total / VIEWS)]
    unnamed x2 -> x1, local copies, waits for them, and re-layouts: 0.01 us -> 2.26 us
where the time goes in v1:
time: 69.8 us; the launch traced here: 69.5 us
  Pallas kernels  67.3 us (96%)
  local copies, waits for them, and re-layouts  2.26 us (3%)
    pallas_call x1, Pallas kernels, body(): pl.pallas_call(lambda *refs: kernel(nx, ny, *refs), out_shape=jax.ShapeDt...  67.3 us
    unnamed x1, local copies, waits for them, and re-layouts  2.26 us

profile of v1, /device:TPU:1, one launch (start us, length us, event | category | flops | bytes accessed | tf_op | source)
XLA Modules:
  0.0 69.5 jit_solution(1316815271221516265)
XLA Ops:
  0.0 67.3 %richardson_lucy.1 = f32[64,32,128]{2,1,0:T(8,128)} custom-call(f32[6,3,31]{2,1,0:T(4,128)} %refs_0_.1, s32[384]{0:T(512)} %refs_1_.1, s32[384]{0:T(512)} %refs_2_.1, f32[64,32,128]{2,1,0:T(8,128)} %refs_3_.1, bf16[384,32,128]{2,1,0:T(8,128)(2,1)} %refs_4_.1), custom_call_target="tpu_custom_call" | custom-call | tf_op jit(solution)/shard_map/richardson_lucy/pallas_call | solution.py:373
  67.3 2.3 %copy.7 = f32[64,32,128]{2,1,0:T(8,128)} copy(f32[64,32,128]{2,1,0:T(8,128)} %richardson_lucy.1) | data formatting | bytes 2097152

commit v2 on v1

--- a/solution.py
+++ b/solution.py
@@ -41,19 +41,42 @@
     return pltpu.roll(wide, shift, 1, stride=1, stride_axis=0)
 
 
+def guarded(condition, action):
+    if condition is None:
+        action()
+    else:
+        pl.when(condition)(action)
+
+
+class Send:
+    def __init__(self, src, dst, send_sem, recv_sem, target, sends=None, receives=None):
+        self.copy = pltpu.make_async_remote_copy(
+            src_ref=src, dst_ref=dst, send_sem=send_sem, recv_sem=recv_sem,
+            device_id=target, device_id_type=MESH,
+        )
+        self.sends, self.receives = sends, receives
+        guarded(sends, self.copy.start)
+
+    def wait_recv(self):
+        guarded(self.receives, self.copy.wait_recv)
+
+    def wait_send(self):
+        guarded(self.sends, self.copy.wait_send)
+
+
 def lanes(a, b):
     return jnp.concatenate([a, b], axis=1)
 
 
 def kernel(
     nx, ny,
-    taps_ref, owner_ref, offset_ref, est_hbm, tiles_hbm,
+    taps_hbm, owner_hbm, offset_hbm, est_hbm, tiles_hbm,
     out_ref,
     est_v, tiles_v, packed, arrived, ext, blurred, recip, quot, back_rows,
     center, side_out, side_in, row_out, row_in,
-    kpad, row_fwd, row_bwd, col_fwd, col_bwd, depth_fwd, depth_bwd,
+    taps_ref, owner_ref, offset_ref, kpad, row_fwd, row_bwd, col_fwd, col_bwd, depth_fwd, depth_bwd,
     index_v, index_s, slot_v, slot_s, label_out, label_in,
-    load_sem, index_sem, store_sem,
+    load_sem, index_sem, relay,
     halo_send, halo_recv, tile_send, tile_recv, label_send, label_recv,
     side_send, side_recv, row_send, row_recv,
 ):
@@ -65,40 +88,47 @@
     def step_of(group):
         return group // 3 - 1, group % 3 - 1
 
+    barrier = pltpu.get_barrier_semaphore()
+    for group in (5, 3, 1, 7):
+        pl.semaphore_signal(barrier, inc=1, device_id=device(*step_of(group)), device_id_type=MESH)
+
     load_est = pltpu.make_async_copy(est_hbm, est_v, load_sem.at[0])
+    load_owner = pltpu.make_async_copy(owner_hbm, owner_ref, load_sem.at[2])
+    load_offset = pltpu.make_async_copy(offset_hbm, offset_ref, load_sem.at[3])
     load_tiles = pltpu.make_async_copy(tiles_hbm, tiles_v, load_sem.at[1])
+    load_taps = pltpu.make_async_copy(taps_hbm, taps_ref, load_sem.at[4])
     load_est.start()
+    load_owner.start()
+    load_offset.start()
     load_tiles.start()
-
-    barrier = pltpu.get_barrier_semaphore()
-    for group in ORDER:
-        pl.semaphore_signal(barrier, inc=1, device_id=device(*step_of(group)), device_id_type=MESH)
+    load_taps.start()
 
     load_est.wait()
     zero_row = jnp.zeros((XCOLS, DEPTH), BF16)
     ext[0] = zero_row
     ext[XROWS - 1] = zero_row
     ext[HALO:HALO + ROWS, HALO:HALO + COLS, :] = est_v[...].astype(BF16)
-    pl.semaphore_wait(barrier, len(ORDER))
-
-    def send_halo(group, src, dst):
-        copy = pltpu.make_async_remote_copy(
-            src_ref=ext.at[src],
-            dst_ref=ext.at[dst],
-            send_sem=halo_send.at[group],
-            recv_sem=halo_recv.at[group],
-            device_id=device(*step_of(group)),
-            device_id_type=MESH,
+    pl.semaphore_wait(barrier, 4)
+
+    up, down, right, left = gx != nx - 1, gx != 0, gy != ny - 1, gy != 0
+
+    def send_halo(group, src, dst, sends, receives):
+        return Send(
+            ext.at[src], ext.at[dst], halo_send.at[group], halo_recv.at[group],
+            device(*step_of(group)), sends, receives,
         )
-        copy.start()
-        return copy
 
     inner = slice(HALO, HALO + ROWS)
     halo_copies = [
-        send_halo(5, (inner, slice(COLS, COLS + HALO)), (inner, slice(0, HALO))),
-        send_halo(3, (inner, slice(HALO, 2 * HALO)), (inner, slice(HALO + COLS, XCOLS))),
+        send_halo(5, (inner, slice(COLS, COLS + HALO)), (inner, slice(0, HALO)), right, left),
+        send_halo(3, (inner, slice(HALO, 2 * HALO)), (inner, slice(HALO + COLS, XCOLS)), left, right),
     ]
 
+    for group in (5, 3):
+        pl.semaphore_signal(relay, inc=1, device_id=device(*step_of(group)), device_id_type=MESH)
+
+    load_owner.wait()
+    load_offset.wait()
     owner = owner_ref[...].reshape(1, TILES)
     shift = ny.bit_length() - 1
 
@@ -125,39 +155,31 @@
         label_out[group] = jnp.broadcast_to(label[:, group * 128:(group + 1) * 128], (8, 128))
     load_index = pltpu.make_async_copy(index_v, index_s, index_sem.at[0])
     load_index.start()
-    label_copies = []
-    for group in ORDER:
-        copy = pltpu.make_async_remote_copy(
-            src_ref=label_out.at[group],
-            dst_ref=label_in.at[group],
-            send_sem=label_send.at[group],
-            recv_sem=label_recv.at[group],
-            device_id=device(*step_of(group)),
-            device_id_type=MESH,
-        )
-        copy.start()
-        label_copies.append(copy)
     label_in[OWN] = label_out[OWN]
 
     load_index.wait()
     load_tiles.wait()
-    tile_copies = []
+    label_copies, tile_copies = [], []
     for group in ORDER:
         def pack(r, carry, group=group):
             packed[group * SLOTS + r] = tiles_v[index_s[group, r]]
             return carry
 
         lax.fori_loop(0, SLOTS, pack, 0, unroll=8)
-        copy = pltpu.make_async_remote_copy(
-            src_ref=packed.at[group * SLOTS:(group + 1) * SLOTS],
-            dst_ref=arrived.at[group * SLOTS:(group + 1) * SLOTS],
-            send_sem=tile_send.at[group],
-            recv_sem=tile_recv.at[group],
-            device_id=device(*step_of(group)),
-            device_id_type=MESH,
-        )
-        copy.start()
-        tile_copies.append(copy)
+        if group == ORDER[2]:
+            pl.semaphore_wait(relay, 2)
+            label_copies = [
+                Send(
+                    label_out.at[other], label_in.at[other], label_send.at[other], label_recv.at[other],
+                    device(*step_of(other)),
+                )
+                for other in ORDER
+            ]
+        slots = slice(group * SLOTS, (group + 1) * SLOTS)
+        tile_copies.append(Send(
+            packed.at[slots], arrived.at[slots], tile_send.at[group], tile_recv.at[group],
+            device(*step_of(group)),
+        ))
 
     def keep(r, carry):
         arrived[OWN * SLOTS + r] = tiles_v[index_s[OWN, r]]
@@ -175,10 +197,11 @@
     clear(gy == 0, inner, slice(0, HALO))
     clear(gy == ny - 1, inner, slice(HALO + COLS, XCOLS))
     row_halos = [
-        send_halo(7, slice(ROWS + 1, ROWS + HALO), slice(1, HALO)),
-        send_halo(1, slice(HALO, 2 * HALO - 1), slice(HALO + ROWS, XROWS - 1)),
+        send_halo(7, slice(ROWS + 1, ROWS + HALO), slice(1, HALO), up, down),
+        send_halo(1, slice(HALO, 2 * HALO - 1), slice(HALO + ROWS, XROWS - 1), down, up),
     ]
 
+    load_taps.wait()
     kpad[...] = jnp.zeros_like(kpad)
     kpad[:, 0:3, 0:TAPS] = taps_ref[...]
     spread = onehot((iota((256, 16), 0) >> 4) == iota((256, 16), 1))
@@ -306,31 +329,22 @@
 
         lax.fori_loop(0, 8, cols_back, 0, unroll=8)
         dx = -1 if band == 0 else 1 if band == BANDS - 1 else 0
+        sends, receives = {0: (None, None), -1: (down, up), 1: (up, down)}[dx]
         for side in range(2):
-            copy = pltpu.make_async_remote_copy(
-                src_ref=side_out.at[band, side],
-                dst_ref=side_in.at[band, side],
-                send_sem=side_send.at[band, side],
-                recv_sem=side_recv.at[band, side],
-                device_id=device(dx, 2 * side - 1),
-                device_id_type=MESH,
-            )
-            copy.start()
-            side_copies.append(copy)
+            out_of, into = (left, right) if side == 0 else (right, left)
+            if dx != 0:
+                out_of, into = jnp.logical_and(out_of, sends), jnp.logical_and(into, receives)
+            side_copies.append(Send(
+                side_out.at[band, side], side_in.at[band, side],
+                side_send.at[band, side], side_recv.at[band, side],
+                device(dx, 2 * side - 1), out_of, into,
+            ))
         if dx != 0:
             end = band // (BANDS - 1)
-            copy = pltpu.make_async_remote_copy(
-                src_ref=row_out.at[end],
-                dst_ref=row_in.at[end],
-                send_sem=row_send.at[end],
-                recv_sem=row_recv.at[end],
-                device_id=device(dx, 0),
-                device_id_type=MESH,
-            )
-            copy.start()
-            row_copies.append(copy)
-
-    from_right, from_left = gy != ny - 1, gy != 0
+            row_copies.append(Send(
+                row_out.at[end], row_in.at[end], row_send.at[end], row_recv.at[end],
+                device(dx, 0), sends, receives,
+            ))
 
     def sides(band, inside):
         for copy in side_copies[2 * band:2 * band + 2]:
@@ -338,29 +352,21 @@
         low = side_in[band, 1].astype(F32)
         high = side_in[band, 0].astype(F32)
         return jnp.concatenate([
-            jnp.where(jnp.logical_and(from_left, inside), low, 0.0),
-            jnp.where(jnp.logical_and(from_right, inside), high, 0.0),
+            jnp.where(jnp.logical_and(left, inside), low, 0.0),
+            jnp.where(jnp.logical_and(right, inside), high, 0.0),
         ], axis=1)
 
-    stores = []
     for c in (1, 2, 0, 3):
         rows = slice(16 * c, 16 * c + 16)
         total = center[rows] + sides(c + 1, True)
         if c == 0:
-            inside = gx != 0
             row_copies[1].wait_recv()
-            total = total + sides(BANDS - 1, inside) + jnp.where(inside, row_in[1].astype(F32), 0.0)
+            total = total + sides(BANDS - 1, down) + jnp.where(down, row_in[1].astype(F32), 0.0)
         if c == TILE_BANDS - 1:
-            inside = gx != nx - 1
             row_copies[0].wait_recv()
-            total = total + sides(0, inside) + jnp.where(inside, row_in[0].astype(F32), 0.0)
-        center[rows] = est_v[rows] * (total * (1.0 / VIEWS))
-        store = pltpu.make_async_copy(center.at[rows], out_ref.at[rows], store_sem.at[c])
-        store.start()
-        stores.append(store)
-
-    for store in stores:
-        store.wait()
+            total = total + sides(0, up) + jnp.where(up, row_in[0].astype(F32), 0.0)
+        out_ref[rows] = est_v[rows] * (total * (1.0 / VIEWS))
+
     for copy in halo_copies + label_copies + tile_copies + side_copies + row_copies:
         copy.wait_send()
 
@@ -372,9 +378,9 @@
     dma = pltpu.SemaphoreType.DMA
     return pl.pallas_call(
         lambda *refs: kernel(nx, ny, *refs),
-        out_shape=jax.ShapeDtypeStruct((ROWS, COLS, DEPTH), F32),
-        in_specs=[vmem, vmem, vmem, anywhere, anywhere],
-        out_specs=anywhere,
+        out_shape=pltpu.VMEM((ROWS, COLS, DEPTH), F32),
+        in_specs=[anywhere] * 5,
+        out_specs=vmem,
         scratch_shapes=[
             pltpu.VMEM((ROWS, COLS, DEPTH), F32),
             pltpu.VMEM((TILES, COLS, DEPTH), BF16),
@@ -390,6 +396,9 @@
             pltpu.VMEM((BANDS, 2, 16, HALO, DEPTH), BF16),
             pltpu.VMEM((2, 16, COLS, DEPTH), BF16),
             pltpu.VMEM((2, 16, COLS, DEPTH), BF16),
+            pltpu.VMEM((VIEWS, 3, TAPS), F32),
+            pltpu.VMEM((TILES,), I32),
+            pltpu.VMEM((TILES,), I32),
             pltpu.VMEM((VIEWS, 8, 128), F32),
             pltpu.VMEM((VIEWS, 256, 768), BF16),
             pltpu.VMEM((VIEWS, 256, 768), BF16),
@@ -403,7 +412,7 @@
             pltpu.SMEM((8, 128), I32),
             pltpu.VMEM((9, 8, 128), I32),
             pltpu.VMEM((9, 8, 128), I32),
-            dma((2,)), dma((2,)), dma((4,)),
+            dma((5,)), dma((2,)), pltpu.SemaphoreType.REGULAR,
             dma((9,)), dma((9,)), dma((9,)), dma((9,)), dma((9,)), dma((9,)),
             dma((BANDS, 2)), dma((BANDS, 2)), dma((2,)), dma((2,)),
         ],

time: 69.8 us -> 61.5 us (0.88)
  Pallas kernels: 67.3 us -> 60.4 us
  local copies, waits for them, and re-layouts: 2.26 us -> 0.97 us
    pallas_call x1, Pallas kernels: 67.3 us -> 60.4 us  [body(): pl.pallas_call(lambda *refs: kernel(nx, ny, *refs), out_shape=pltpu.VMEM(...]
    unnamed x1, local copies, waits for them, and re-layouts: 2.26 us -> 0.97 us
where the time goes in v2:
time: 61.5 us; the launch traced here: 61.4 us
  Pallas kernels  60.4 us (98%)
  local copies, waits for them, and re-layouts  0.97 us (2%)
    pallas_call x1, Pallas kernels, body(): pl.pallas_call(lambda *refs: kernel(nx, ny, *refs), out_shape=pltpu.VMEM(...  60.4 us

profile of v2, /device:TPU:1, one launch (start us, length us, event | category | flops | bytes accessed | tf_op | source)
XLA Modules:
  0.0 61.4 jit_solution(3928995203601507378)
XLA Ops:
  0.0 60.4 %richardson_lucy.1 = f32[64,32,128]{2,1,0:T(8,128)S(1)} custom-call(f32[6,3,31]{2,1,0:T(4,128)} %refs_0_.1, s32[384]{0:T(512)} %refs_1_.1, s32[384]{0:T(512)} %refs_2_.1, f32[64,32,128]{2,1,0:T(8,128)} %refs_3_.1, bf16[384,32,128]{2,1,0:T(8,128)(2,1)} %refs_4_.1), custom_call_target="tpu_custom_call" | custom-call | tf_op jit(solution)/shard_map/richardson_lucy/pallas_call | solution.py:379
  60.4 1.0 %copy.7 = f32[64,32,128]{2,1,0:T(8,128)} copy(f32[64,32,128]{2,1,0:T(8,128)S(1)} %richardson_lucy.1) | data formatting | bytes 2097152

commit v3 on v2

--- a/solution.py
+++ b/solution.py
@@ -14,8 +14,9 @@
 HALO = 16
 XROWS, XCOLS = ROWS + 2 * HALO, COLS + 2 * HALO
 SLOTS = 64
+WIDE = 640
 OWN = 4
-ORDER = (5, 3, 2, 0, 8, 6, 1, 7)
+ORDER = (8, 6, 2, 0, 7, 1, 5, 3)
 BANDS = XROWS // 16
 TILE_BANDS = ROWS // 16
 
@@ -103,30 +104,6 @@
     load_tiles.start()
     load_taps.start()
 
-    load_est.wait()
-    zero_row = jnp.zeros((XCOLS, DEPTH), BF16)
-    ext[0] = zero_row
-    ext[XROWS - 1] = zero_row
-    ext[HALO:HALO + ROWS, HALO:HALO + COLS, :] = est_v[...].astype(BF16)
-    pl.semaphore_wait(barrier, 4)
-
-    up, down, right, left = gx != nx - 1, gx != 0, gy != ny - 1, gy != 0
-
-    def send_halo(group, src, dst, sends, receives):
-        return Send(
-            ext.at[src], ext.at[dst], halo_send.at[group], halo_recv.at[group],
-            device(*step_of(group)), sends, receives,
-        )
-
-    inner = slice(HALO, HALO + ROWS)
-    halo_copies = [
-        send_halo(5, (inner, slice(COLS, COLS + HALO)), (inner, slice(0, HALO)), right, left),
-        send_halo(3, (inner, slice(HALO, 2 * HALO)), (inner, slice(HALO + COLS, XCOLS)), left, right),
-    ]
-
-    for group in (5, 3):
-        pl.semaphore_signal(relay, inc=1, device_id=device(*step_of(group)), device_id_type=MESH)
-
     load_owner.wait()
     load_offset.wait()
     owner = owner_ref[...].reshape(1, TILES)
@@ -139,8 +116,8 @@
     members = jnp.where(iota((16, TILES), 0) == group_of, 1.0, 0.0)
     before = onehot(iota((TILES, TILES), 0) < iota((TILES, TILES), 1))
     rank = jnp.sum(members * dot(members.astype(BF16), before), axis=0, keepdims=True)
-    place = group_of * 128 + rank.astype(I32)
-    picks = onehot(iota((9 * 128, TILES), 0) == place)
+    place = group_of * SLOTS + rank.astype(I32)
+    picks = onehot(iota((WIDE, TILES), 0) == place)
     number = iota((8, TILES), 1)
     row = iota((8, TILES), 0)
     offset = jnp.broadcast_to(offset_ref[...].reshape(1, TILES), (8, TILES))
@@ -150,11 +127,37 @@
     source = jnp.clip((found[0:1] * 16.0 + found[1:2]).astype(I32), 0, TILES - 1)
     label = (found[2:3] * 16.0 + found[3:4] + (found[4:5] - 1.0) * 1024.0).astype(I32)
     index_v[...] = jnp.zeros_like(index_v)
-    for group in range(9):
-        index_v[group:group + 1, :] = source[:, group * 128:(group + 1) * 128]
-        label_out[group] = jnp.broadcast_to(label[:, group * 128:(group + 1) * 128], (8, 128))
+    for n in range(WIDE // 128):
+        index_v[n:n + 1, :] = source[:, n * 128:(n + 1) * 128]
+        for group in range(2 * n, min(2 * n + 2, 9)):
+            label_out[group] = jnp.broadcast_to(label[:, n * 128:(n + 1) * 128], (8, 128))
     load_index = pltpu.make_async_copy(index_v, index_s, index_sem.at[0])
     load_index.start()
+
+    load_est.wait()
+    zero_row = jnp.zeros((XCOLS, DEPTH), BF16)
+    ext[0] = zero_row
+    ext[XROWS - 1] = zero_row
+    ext[HALO:HALO + ROWS, HALO:HALO + COLS, :] = est_v[...].astype(BF16)
+    pl.semaphore_wait(barrier, 4)
+
+    up, down, right, left = gx != nx - 1, gx != 0, gy != ny - 1, gy != 0
+
+    def send_halo(group, src, dst, sends, receives):
+        return Send(
+            ext.at[src], ext.at[dst], halo_send.at[group], halo_recv.at[group],
+            device(*step_of(group)), sends, receives,
+        )
+
+    inner = slice(HALO, HALO + ROWS)
+    halo_copies = [
+        send_halo(5, (inner, slice(COLS, COLS + HALO)), (inner, slice(0, HALO)), right, left),
+        send_halo(3, (inner, slice(HALO, 2 * HALO)), (inner, slice(HALO + COLS, XCOLS)), left, right),
+    ]
+
+    for group in (5, 3):
+        pl.semaphore_signal(relay, inc=1, device_id=device(*step_of(group)), device_id_type=MESH)
+
     label_in[OWN] = label_out[OWN]
 
     load_index.wait()
@@ -162,11 +165,11 @@
     label_copies, tile_copies = [], []
     for group in ORDER:
         def pack(r, carry, group=group):
-            packed[group * SLOTS + r] = tiles_v[index_s[group, r]]
+            packed[group * SLOTS + r] = tiles_v[index_s[group // 2, group % 2 * SLOTS + r]]
             return carry
 
         lax.fori_loop(0, SLOTS, pack, 0, unroll=8)
-        if group == ORDER[2]:
+        if group == ORDER[0]:
             pl.semaphore_wait(relay, 2)
             label_copies = [
                 Send(
@@ -182,7 +185,7 @@
         ))
 
     def keep(r, carry):
-        arrived[OWN * SLOTS + r] = tiles_v[index_s[OWN, r]]
+        arrived[OWN * SLOTS + r] = tiles_v[index_s[OWN // 2, OWN % 2 * SLOTS + r]]
         return carry
 
     lax.fori_loop(0, SLOTS, keep, 0, unroll=8)
@@ -266,12 +269,17 @@
 
     for copy in label_copies:
         copy.wait_recv()
-    labels = jnp.concatenate([label_in[group][0:1] for group in range(9)], axis=1)
-    where_is = onehot(iota((TILES, 9 * 128), 0) == labels)
-    place_no = iota((8, 9 * 128), 1)
-    place_digits = jnp.where(iota((8, 9 * 128), 0) == 0, place_no >> 7, place_no & 127)
-    got = dot_nt(place_digits.astype(F32).astype(BF16), where_is)
-    slots = jnp.clip((got[0:1] * float(SLOTS) + got[1:2]).astype(I32), 0, 9 * SLOTS - 1)
+    first_half = iota((1, 128), 1) < SLOTS
+    nobody = jnp.full((1, 128), -1, I32)
+    labels = jnp.concatenate([
+        jnp.where(first_half, label_in[2 * n][0:1], label_in[2 * n + 1][0:1] if 2 * n + 1 < 9 else nobody)
+        for n in range(WIDE // 128)
+    ], axis=1)
+    where_is = onehot(iota((TILES, WIDE), 0) == labels)
+    slot_no = iota((8, WIDE), 1)
+    slot_digits = jnp.where(iota((8, WIDE), 0) == 0, slot_no >> 4, slot_no & 15)
+    got = dot_nt(slot_digits.astype(F32).astype(BF16), where_is)
+    slots = jnp.clip((got[0:1] * 16.0 + got[1:2]).astype(I32), 0, 9 * SLOTS - 1)
     slot_v[...] = jnp.zeros_like(slot_v)
     for n in range(3):
         slot_v[n:n + 1, :] = slots[:, 128 * n:128 * (n + 1)]
@@ -356,7 +364,7 @@
             jnp.where(jnp.logical_and(right, inside), high, 0.0),
         ], axis=1)
 
-    for c in (1, 2, 0, 3):
+    for c in (1, 2, 3, 0):
         rows = slice(16 * c, 16 * c + 16)
         total = center[rows] + sides(c + 1, True)
         if c == 0:
@@ -406,8 +414,8 @@
             pltpu.VMEM((XCOLS, VIEWS * COLS), BF16),
             pltpu.VMEM((VIEWS // 2, 256, 256), BF16),
             pltpu.VMEM((VIEWS // 2, 256, 256), BF16),
-            pltpu.VMEM((16, 128), I32),
-            pltpu.SMEM((16, 128), I32),
+            pltpu.VMEM((8, 128), I32),
+            pltpu.SMEM((8, 128), I32),
             pltpu.VMEM((8, 128), I32),
             pltpu.SMEM((8, 128), I32),
             pltpu.VMEM((9, 8, 128), I32),

time: 61.5 us -> 59.7 us (0.971)
  Pallas kernels: 60.4 us -> 58.6 us
    pallas_call x1, Pallas kernels: 60.4 us -> 58.6 us  [body(): pl.pallas_call(lambda *refs: kernel(nx, ny, *refs), out_shape=pltpu.VMEM(...]
where the time goes in v3:
time: 59.7 us; the launch traced here: 59.6 us
  Pallas kernels  58.6 us (98%)
  local copies, waits for them, and re-layouts  0.97 us (2%)
    pallas_call x1, Pallas kernels, body(): pl.pallas_call(lambda *refs: kernel(nx, ny, *refs), out_shape=pltpu.VMEM(...  58.6 us

profile of v3, /device:TPU:1, one launch (start us, length us, event | category | flops | bytes accessed | tf_op | source)
XLA Modules:
  0.0 59.6 jit_solution(5537817000125297138)
XLA Ops:
  0.0 58.6 %richardson_lucy.1 = f32[64,32,128]{2,1,0:T(8,128)S(1)} custom-call(f32[6,3,31]{2,1,0:T(4,128)} %refs_0_.1, s32[384]{0:T(512)} %refs_1_.1, s32[384]{0:T(512)} %refs_2_.1, f32[64,32,128]{2,1,0:T(8,128)} %refs_3_.1, bf16[384,32,128]{2,1,0:T(8,128)(2,1)} %refs_4_.1), custom_call_target="tpu_custom_call" | custom-call | tf_op jit(solution)/shard_map/richardson_lucy/pallas_call | solution.py:387
  58.6 1.0 %copy.7 = f32[64,32,128]{2,1,0:T(8,128)} copy(f32[64,32,128]{2,1,0:T(8,128)S(1)} %richardson_lucy.1) | data formatting | bytes 2097152

commit v4 on v3

--- a/solution.py
+++ b/solution.py
@@ -289,40 +289,47 @@
     for copy in tile_copies:
         copy.wait_recv()
 
-    side_copies, row_copies = [], []
-    for band in range(BANDS):
-        if band < TILE_BANDS:
-            def quotients(pair, carry, band=band):
-                tiles = []
-                for i in range(16):
-                    halves = []
-                    for e in range(2):
-                        at = slot_s[pair, 64 * e + 16 * band + i]
-                        value = arrived[at].astype(F32) * recip[2 * pair + e, 16 * band + i]
-                        halves.append(value.astype(BF16))
-                    tiles.append(lanes(halves[0], halves[1]))
-                out = dot(jnp.concatenate(tiles, axis=0), depth_bwd[pair]).astype(BF16)
+    def quotients_of(band):
+        def quotients(pair, carry):
+            tiles = []
+            for i in range(16):
+                halves = []
                 for e in range(2):
-                    quot[2 * pair + e, 16 * band:16 * band + 16] = out[
-                        :, 128 * e:128 * e + 128].reshape(16, COLS, DEPTH)
-                return carry
-
-            lax.fori_loop(0, 3, quotients, 0, unroll=3)
+                    at = slot_s[pair, 64 * e + 16 * band + i]
+                    value = arrived[at].astype(F32) * recip[2 * pair + e, 16 * band + i]
+                    halves.append(value.astype(BF16))
+                tiles.append(lanes(halves[0], halves[1]))
+            out = dot(jnp.concatenate(tiles, axis=0), depth_bwd[pair]).astype(BF16)
+            for e in range(2):
+                quot[2 * pair + e, 16 * band:16 * band + 16] = out[
+                    :, 128 * e:128 * e + 128].reshape(16, COLS, DEPTH)
+            return carry
+
+        lax.fori_loop(0, 3, quotients, 0, unroll=3)
+
+    def rows_of(band):
         s0, s1 = max(0, band - 2), min(TILE_BANDS - 1, band)
         w0, w1 = 256 * (2 - (band - s0)), 256 * (3 - (band - s1))
-
-        def rows_back(v, carry, s0=s0, s1=s1, w0=w0, w1=w1):
+        buffer = band % 2
+
+        def rows_back(v, carry):
             block = quot[v, 16 * s0:16 * (s1 + 1)]
             both = lanes(block[:, 0:16].reshape(w1 - w0, DEPTH), block[:, 16:32].reshape(w1 - w0, DEPTH))
             out = dot(row_bwd[v, :, w0:w1], both).astype(BF16)
-            back_rows[:, v, 0:16, :] = out[:, 0:128].reshape(16, 16, DEPTH)
-            back_rows[:, v, 16:32, :] = out[:, 128:256].reshape(16, 16, DEPTH)
+            back_rows[buffer, :, v, 0:16, :] = out[:, 0:128].reshape(16, 16, DEPTH)
+            back_rows[buffer, :, v, 16:32, :] = out[:, 128:256].reshape(16, 16, DEPTH)
             return carry
 
         lax.fori_loop(0, VIEWS, rows_back, 0, unroll=6)
 
-        def cols_back(p, carry, band=band):
-            both = lanes(back_rows[2 * p].reshape(VIEWS * COLS, DEPTH), back_rows[2 * p + 1].reshape(VIEWS * COLS, DEPTH))
+    def cols_of(band):
+        buffer = band % 2
+
+        def cols_back(p, carry):
+            both = lanes(
+                back_rows[buffer, 2 * p].reshape(VIEWS * COLS, DEPTH),
+                back_rows[buffer, 2 * p + 1].reshape(VIEWS * COLS, DEPTH),
+            )
             out = dot(col_bwd[...], both)
             for e in range(2):
                 one = out[:, 128 * e:128 * e + 128]
@@ -336,26 +343,56 @@
             return carry
 
         lax.fori_loop(0, 8, cols_back, 0, unroll=8)
+
+    side_copies, row_copies = {}, {}
+
+    def send_of(band):
         dx = -1 if band == 0 else 1 if band == BANDS - 1 else 0
         sends, receives = {0: (None, None), -1: (down, up), 1: (up, down)}[dx]
+        side_copies[band] = []
         for side in range(2):
             out_of, into = (left, right) if side == 0 else (right, left)
             if dx != 0:
                 out_of, into = jnp.logical_and(out_of, sends), jnp.logical_and(into, receives)
-            side_copies.append(Send(
+            side_copies[band].append(Send(
                 side_out.at[band, side], side_in.at[band, side],
                 side_send.at[band, side], side_recv.at[band, side],
                 device(dx, 2 * side - 1), out_of, into,
             ))
         if dx != 0:
             end = band // (BANDS - 1)
-            row_copies.append(Send(
+            row_copies[end] = Send(
                 row_out.at[end], row_in.at[end], row_send.at[end], row_recv.at[end],
                 device(dx, 0), sends, receives,
-            ))
+            )
+
+    quotients_of(0)
+    rows_of(0)
+    quotients_of(1)
+    cols_of(0)
+    send_of(0)
+    rows_of(1)
+    quotients_of(2)
+    cols_of(1)
+    send_of(1)
+    rows_of(2)
+    quotients_of(3)
+    cols_of(2)
+    send_of(2)
+    rows_of(3)
+    cols_of(3)
+    send_of(3)
+    rows_of(4)
+    cols_of(4)
+    send_of(4)
+    rows_of(5)
+    cols_of(5)
+    send_of(5)
+    for copy in halo_copies + label_copies + tile_copies:
+        copy.wait_send()
 
     def sides(band, inside):
-        for copy in side_copies[2 * band:2 * band + 2]:
+        for copy in side_copies[band]:
             copy.wait_recv()
         low = side_in[band, 1].astype(F32)
         high = side_in[band, 0].astype(F32)
@@ -368,6 +405,8 @@
         rows = slice(16 * c, 16 * c + 16)
         total = center[rows] + sides(c + 1, True)
         if c == 0:
+            for copy in sum((side_copies[band] for band in range(BANDS - 1)), []):
+                copy.wait_send()
             row_copies[1].wait_recv()
             total = total + sides(BANDS - 1, down) + jnp.where(down, row_in[1].astype(F32), 0.0)
         if c == TILE_BANDS - 1:
@@ -375,7 +414,7 @@
             total = total + sides(0, up) + jnp.where(up, row_in[0].astype(F32), 0.0)
         out_ref[rows] = est_v[rows] * (total * (1.0 / VIEWS))
 
-    for copy in halo_copies + label_copies + tile_copies + side_copies + row_copies:
+    for copy in side_copies[BANDS - 1] + list(row_copies.values()):
         copy.wait_send()
 
 
@@ -398,7 +437,7 @@
             pltpu.VMEM((XROWS, VIEWS, COLS, DEPTH), BF16),
             pltpu.VMEM((VIEWS, ROWS, COLS, DEPTH), F32),
             pltpu.VMEM((VIEWS, ROWS, COLS, DEPTH), BF16),
-            pltpu.VMEM((16, VIEWS, COLS, DEPTH), BF16),
+            pltpu.VMEM((2, 16, VIEWS, COLS, DEPTH), BF16),
             pltpu.VMEM((ROWS, COLS, DEPTH), F32),
             pltpu.VMEM((BANDS, 2, 16, HALO, DEPTH), BF16),
             pltpu.VMEM((BANDS, 2, 16, HALO, DEPTH), BF16),

time: 59.7 us -> 59.3 us (level)
  no operation moved by 1% of the time
where the time goes in v4:
time: 59.3 us; the launch traced here: 59.2 us
  Pallas kernels  58.2 us (98%)
  local copies, waits for them, and re-layouts  0.97 us (2%)
    pallas_call x1, Pallas kernels, body(): pl.pallas_call(lambda *refs: kernel(nx, ny, *refs), out_shape=pltpu.VMEM(...  58.2 us

profile of v4, /device:TPU:1, one launch (start us, length us, event | category | flops | bytes accessed | tf_op | source)
XLA Modules:
  0.0 59.2 jit_solution(9367999156164074118)
XLA Ops:
  0.0 58.2 %richardson_lucy.1 = f32[64,32,128]{2,1,0:T(8,128)S(1)} custom-call(f32[6,3,31]{2,1,0:T(4,128)} %refs_0_.1, s32[384]{0:T(512)} %refs_1_.1, s32[384]{0:T(512)} %refs_2_.1, f32[64,32,128]{2,1,0:T(8,128)} %refs_3_.1, bf16[384,32,128]{2,1,0:T(8,128)(2,1)} %refs_4_.1), custom_call_target="tpu_custom_call" | custom-call | tf_op jit(solution)/shard_map/richardson_lucy/pallas_call | solution.py:426
  58.2 1.0 %copy.7 = f32[64,32,128]{2,1,0:T(8,128)} copy(f32[64,32,128]{2,1,0:T(8,128)S(1)} %richardson_lucy.1) | data formatting | bytes 2097152

commit v5 on v4

--- a/solution.py
+++ b/solution.py
@@ -368,15 +368,18 @@
 
     quotients_of(0)
     rows_of(0)
-    quotients_of(1)
+    quotients_of(3)
     cols_of(0)
     send_of(0)
+    rows_of(5)
+    quotients_of(1)
+    cols_of(5)
+    send_of(5)
     rows_of(1)
     quotients_of(2)
     cols_of(1)
     send_of(1)
     rows_of(2)
-    quotients_of(3)
     cols_of(2)
     send_of(2)
     rows_of(3)
@@ -385,9 +388,7 @@
     rows_of(4)
     cols_of(4)
     send_of(4)
-    rows_of(5)
-    cols_of(5)
-    send_of(5)
+
     for copy in halo_copies + label_copies + tile_copies:
         copy.wait_send()
 
@@ -401,11 +402,11 @@
             jnp.where(jnp.logical_and(right, inside), high, 0.0),
         ], axis=1)
 
-    for c in (1, 2, 3, 0):
+    for c in (1, 0, 2, 3):
         rows = slice(16 * c, 16 * c + 16)
         total = center[rows] + sides(c + 1, True)
         if c == 0:
-            for copy in sum((side_copies[band] for band in range(BANDS - 1)), []):
+            for copy in sum((side_copies[band] for band in (0, 1, 2, 3, 5)), []):
                 copy.wait_send()
             row_copies[1].wait_recv()
             total = total + sides(BANDS - 1, down) + jnp.where(down, row_in[1].astype(F32), 0.0)
@@ -414,7 +415,7 @@
             total = total + sides(0, up) + jnp.where(up, row_in[0].astype(F32), 0.0)
         out_ref[rows] = est_v[rows] * (total * (1.0 / VIEWS))
 
-    for copy in side_copies[BANDS - 1] + list(row_copies.values()):
+    for copy in side_copies[TILE_BANDS] + list(row_copies.values()):
         copy.wait_send()
 
 

time: 59.3 us -> 59 us (level); the launches traced: 59.2 us -> 58 us
  Pallas kernels: 58.2 us -> 57 us
    pallas_call x1, Pallas kernels: 58.2 us -> 57 us  [body(): pl.pallas_call(lambda *refs: kernel(nx, ny, *refs), out_shape=pltpu.VMEM(...]
where the time goes in v5:
time: 59 us; the launch traced here: 58 us
  Pallas kernels  57 us (97%)
  local copies, waits for them, and re-layouts  0.97 us (2%)
    pallas_call x1, Pallas kernels, body(): pl.pallas_call(lambda *refs: kernel(nx, ny, *refs), out_shape=pltpu.VMEM(...  57 us

profile of v5, /device:TPU:1, one launch (start us, length us, event | category | flops | bytes accessed | tf_op | source)
XLA Modules:
  0.0 58.0 jit_solution(10178493891583443451)
XLA Ops:
  0.0 57.0 %richardson_lucy.1 = f32[64,32,128]{2,1,0:T(8,128)S(1)} custom-call(f32[6,3,31]{2,1,0:T(4,128)} %refs_0_.1, s32[384]{0:T(512)} %refs_1_.1, s32[384]{0:T(512)} %refs_2_.1, f32[64,32,128]{2,1,0:T(8,128)} %refs_3_.1, bf16[384,32,128]{2,1,0:T(8,128)(2,1)} %refs_4_.1), custom_call_target="tpu_custom_call" | custom-call | tf_op jit(solution)/shard_map/richardson_lucy/pallas_call | solution.py:427
  57.0 1.0 %copy.7 = f32[64,32,128]{2,1,0:T(8,128)} copy(f32[64,32,128]{2,1,0:T(8,128)S(1)} %richardson_lucy.1) | data formatting | bytes 2097152

commit v6 on v4

--- a/solution.py
+++ b/solution.py
@@ -162,27 +162,35 @@
 
     load_index.wait()
     load_tiles.wait()
-    label_copies, tile_copies = [], []
-    for group in ORDER:
-        def pack(r, carry, group=group):
+    tile_copies = []
+    away = 2 * (gx % 2) - 1
+
+    def group_at(dx, dy):
+        return (dx + 1) * 3 + dy + 1
+
+    def send_tiles(dx, dy):
+        group = group_at(dx, dy)
+
+        def pack(r, carry):
             packed[group * SLOTS + r] = tiles_v[index_s[group // 2, group % 2 * SLOTS + r]]
             return carry
 
         lax.fori_loop(0, SLOTS, pack, 0, unroll=8)
-        if group == ORDER[0]:
-            pl.semaphore_wait(relay, 2)
-            label_copies = [
-                Send(
-                    label_out.at[other], label_in.at[other], label_send.at[other], label_recv.at[other],
-                    device(*step_of(other)),
-                )
-                for other in ORDER
-            ]
-        slots = slice(group * SLOTS, (group + 1) * SLOTS)
+        slots = pl.ds(group * SLOTS, SLOTS)
         tile_copies.append(Send(
-            packed.at[slots], arrived.at[slots], tile_send.at[group], tile_recv.at[group],
-            device(*step_of(group)),
+            packed.at[slots], arrived.at[slots], tile_send.at[group], tile_recv.at[group], device(dx, dy),
         ))
+
+    pl.semaphore_wait(relay, 2)
+    label_copies = [
+        Send(
+            label_out.at[other], label_in.at[other], label_send.at[other], label_recv.at[other],
+            device(*step_of(other)),
+        )
+        for other in ORDER
+    ]
+    for dy in (1, -1, 0):
+        send_tiles(away, dy)
 
     def keep(r, carry):
         arrived[OWN * SLOTS + r] = tiles_v[index_s[OWN // 2, OWN % 2 * SLOTS + r]]
@@ -233,6 +241,10 @@
         depth_fwd[v // 2, at, at] = dot_nt(eye, depth_t).astype(BF16)
     col_bwd[...] = dot_nt(eye[0:XCOLS], col_fwd[...]).astype(BF16)
 
+    for dy in (1, -1, 0):
+        send_tiles(-away, dy)
+    for dy in (1, -1):
+        send_tiles(0, dy)
     for copy in row_halos:
         copy.wait_recv()
     halo_copies += row_halos

time: 59.3 us -> 59.3 us (level)
  no operation moved by 1% of the time
where the time goes in v6:
time: 59.3 us; the launch traced here: 59.2 us
  Pallas kernels  58.2 us (98%)
  local copies, waits for them, and re-layouts  0.97 us (2%)
    pallas_call x1, Pallas kernels, body(): pl.pallas_call(lambda *refs: kernel(nx, ny, *refs), out_shape=pltpu.VMEM(...  58.2 us

profile of v6, /device:TPU:1, one launch (start us, length us, event | category | flops | bytes accessed | tf_op | source)
XLA Modules:
  0.0 59.2 jit_solution(10954004268359015195)
XLA Ops:
  0.0 58.2 %richardson_lucy.1 = f32[64,32,128]{2,1,0:T(8,128)S(1)} custom-call(f32[6,3,31]{2,1,0:T(4,128)} %refs_0_.1, s32[384]{0:T(512)} %refs_1_.1, s32[384]{0:T(512)} %refs_2_.1, f32[64,32,128]{2,1,0:T(8,128)} %refs_3_.1, bf16[384,32,128]{2,1,0:T(8,128)(2,1)} %refs_4_.1), custom_call_target="tpu_custom_call" | custom-call | tf_op jit(solution)/shard_map/richardson_lucy/pallas_call | solution.py:438
  58.2 1.0 %copy.7 = f32[64,32,128]{2,1,0:T(8,128)} copy(f32[64,32,128]{2,1,0:T(8,128)S(1)} %richardson_lucy.1) | data formatting | bytes 2097152
